TPU v7x, 32 devices: a whole 2x2x4 slice. The times are simulated.
32 devices in a mesh: shot: 2 (over y), tx: 4 (over x, core), ty: 4 (over z).
Axes of the slice: x: 2, y: 2, z: 4, core: 2. Of those that a mesh axis runs over, the one named last changes fastest.
Arguments:
- wave_now: float32 [8, 64, 64, 128], P('shot', 'tx', 'ty'), may hold values from -6 to 6
- wave_prev: float32 [8, 64, 64, 128], P('shot', 'tx', 'ty'), may hold values from -6 to 6
- courant: float32 [64, 64, 128], P('tx', 'ty'), may hold values from 0.02 to 0.3
- rec_index: int32 [4, 4, 512], P('tx', 'ty'), may hold values from 0 to 32767
- rec_history: bfloat16 [8, 8, 4, 4, 512], P('shot', None, 'tx', 'ty'), may hold values from -6 to 6
- green: bfloat16 [2, 8192, 8192], P(None, ('tx', 'ty'), 'shot'), may hold values from -0.046875 to 0.046875
- lag_delay: int32 [2], replicated, may hold values from 1 to 8, as said below
- emit_cells: int32 [4, 4, 8, 512], P('tx', 'ty'), may hold values from 0 to 32767
- emit_weights: float32 [4, 4, 8, 512], P('tx', 'ty'), may hold values from 0.25 to 1
Outputs:
- wave_out: float32 [8, 64, 64, 128], P('shot', 'tx', 'ty')
- wave_last: float32 [8, 64, 64, 128], P('shot', 'tx', 'ty')
- emission: float32 [8, 8, 4, 4, 512], P('shot', None, 'tx', 'ty')
Inputs may be any that keep to these rules, and one draw needn't show every extreme that they name: `lag_delay`: one lag group has delay 8, the other a smaller one.
All inputs are finite; a program needn't handle non-finite values.
Results may differ from a plain program's by a relative error of at most 0.0023.
Values may be sent and summed in bfloat16 or wider, within the bound.
A program may use at most 128 MiB of HBM per device.

v0:
```python
import functools

import jax
import jax.numpy as jnp
from jax import lax
from jax.experimental import pallas as pl
from jax.experimental.pallas import tpu as pltpu
from jax.sharding import PartitionSpec as P

STEPS = 8
HIST = 8
MIB = 1024 * 1024


def wave_kernel(
    n_tx, n_ty, now_ref, prev_ref, cour_ref, ridx_ref,
    last_ref, out_ref, rec_ref,
    field, ysend, yrecv, pick_xy, pick_z,
    load_sem, send_sem, recv_sem,
):
    shots, ext_x, ext_y, depth = now_ref.shape
    tx, ty = lax.axis_index("tx"), lax.axis_index("ty")
    there = (tx > 0, tx < n_tx - 1, ty > 0, ty < n_ty - 1)
    target = ({"tx": tx - 1}, {"tx": tx + 1}, {"ty": ty - 1}, {"ty": ty + 1})

    loads = [
        pltpu.make_async_copy(prev_ref, field.at[0, :, pl.ds(1, ext_x)], load_sem.at[0]),
        pltpu.make_async_copy(now_ref, field.at[1, :, pl.ds(1, ext_x)], load_sem.at[1]),
    ]
    for load in loads:
        load.start()

    barrier = pltpu.get_barrier_semaphore()
    for side in range(4):
        @pl.when(there[side])
        def _():
            pl.semaphore_signal(
                barrier, inc=1, device_id=target[side], device_id_type=pl.DeviceIdType.MESH
            )

    for side in range(4):
        @pl.when(jnp.logical_not(there[side]))
        def _():
            def clear(slot, carry):
                if side < 2:
                    field[slot, :, side * (ext_x + 1)] = jnp.zeros((shots, ext_y, depth), jnp.float32)
                else:
                    yrecv[slot, side - 2] = jnp.zeros((shots, ext_x, 1, depth), jnp.float32)
                return carry
            lax.fori_loop(1, STEPS + 1, clear, 0)

    cells = ridx_ref[...]
    points = cells.shape[1]
    rows = lax.broadcasted_iota(jnp.int32, (ext_x * ext_y, points), 0)
    pick_xy[...] = jnp.where(rows == cells // depth, 1.0, 0.0).astype(jnp.bfloat16)
    deep = lax.broadcasted_iota(jnp.int32, (depth, points), 0)
    pick_z[...] = jnp.where(deep == cells % depth, 1.0, 0.0)

    def copy(slot, side):
        if side < 2:
            src = field.at[slot, :, 1 if side == 0 else ext_x]
            dst = field.at[slot, :, ext_x + 1 if side == 0 else 0]
        else:
            src = ysend.at[slot, side - 2]
            dst = yrecv.at[slot, 3 - side]
        return pltpu.make_async_remote_copy(
            src_ref=src, dst_ref=dst,
            send_sem=send_sem.at[slot, side], recv_sem=recv_sem.at[slot, side ^ 1],
            device_id=target[side], device_id_type=pl.DeviceIdType.MESH,
        )

    def landing(slot, side):
        if side < 2:
            dst = field.at[slot, :, 0 if side == 0 else ext_x + 1]
        else:
            dst = yrecv.at[slot, side - 2]
        return pltpu.make_async_remote_copy(
            src_ref=dst, dst_ref=dst,
            send_sem=send_sem.at[slot, side], recv_sem=recv_sem.at[slot, side],
            device_id=target[side], device_id_type=pl.DeviceIdType.MESH,
        )

    def send(slot):
        for side in range(2):
            @pl.when(there[side])
            def _():
                copy(slot, side).start()
        ysend[slot, 0] = field[slot, :, 1 : ext_x + 1, 0:1, :]
        ysend[slot, 1] = field[slot, :, 1 : ext_x + 1, ext_y - 1 : ext_y, :]
        for side in range(2, 4):
            @pl.when(there[side])
            def _():
                copy(slot, side).start()

    for load in loads:
        load.wait()
    peers = sum(jnp.where(flag, 1, 0) for flag in there)
    pl.semaphore_wait(barrier, peers)
    send(1)

    part = 4 if ext_x % 4 == 0 else 1
    shape = (part, ext_y, depth)
    at_y = lax.broadcasted_iota(jnp.int32, shape, 1)
    at_z = lax.broadcasted_iota(jnp.int32, shape, 2)

    def advance(slot):
        def one_shot(s, carry):
            for x0 in range(0, ext_x, part):
                centre = field[slot, s, x0 + 1 : x0 + 1 + part]
                total = field[slot, s, x0 : x0 + part] + field[slot, s, x0 + 2 : x0 + 2 + part]
                low = jnp.broadcast_to(yrecv[slot, 0, s, x0 : x0 + part], shape)
                high = jnp.broadcast_to(yrecv[slot, 1, s, x0 : x0 + part], shape)
                total += jnp.where(at_y == 0, low, pltpu.roll(centre, 1, 1))
                total += jnp.where(at_y == ext_y - 1, high, pltpu.roll(centre, ext_y - 1, 1))
                total += jnp.where(at_z == 0, 0.0, pltpu.roll(centre, 1, 2))
                total += jnp.where(at_z == depth - 1, 0.0, pltpu.roll(centre, depth - 1, 2))
                before = field[slot - 1, s, x0 + 1 : x0 + 1 + part]
                speed = cour_ref[x0 : x0 + part]
                field[slot + 1, s, x0 + 1 : x0 + 1 + part] = (
                    2.0 * centre - before + speed * (total - 6.0 * centre)
                )
            return carry
        lax.fori_loop(0, shots, one_shot, 0)

    def sample(slot):
        for s in range(shots):
            tile = field[slot, s, 1 : ext_x + 1].reshape(ext_x * ext_y, depth).astype(jnp.bfloat16)
            found = lax.dot_general(
                tile, pick_xy[...], (((0,), (0,)), ((), ())), preferred_element_type=jnp.float32
            )
            rec_ref[slot - 2, s : s + 1, :] = jnp.sum(found * pick_z[...], axis=0, keepdims=True)

    def arrive(slot):
        for side in range(4):
            @pl.when(there[side])
            def _():
                landing(slot, side).wait_recv()

    def step(slot, carry):
        arrive(slot)
        advance(slot)
        send(slot + 1)
        sample(slot + 1)
        return carry

    lax.fori_loop(1, STEPS, step, 0)
    arrive(STEPS)
    advance(STEPS)
    sample(STEPS + 1)
    stores = [
        pltpu.make_async_copy(field.at[STEPS, :, pl.ds(1, ext_x)], last_ref, load_sem.at[0]),
        pltpu.make_async_copy(field.at[STEPS + 1, :, pl.ds(1, ext_x)], out_ref, load_sem.at[1]),
    ]
    for store in stores:
        store.start()

    def drain(slot, carry):
        for side in range(4):
            @pl.when(there[side])
            def _():
                copy(slot, side).wait_send()
        return carry
    lax.fori_loop(1, STEPS + 1, drain, 0)
    for store in stores:
        store.wait()


def run_wave(n_tx, n_ty, wave_now, wave_prev, courant, ridx):
    shots, ext_x, ext_y, depth = wave_now.shape
    points = ridx.shape[1]
    whole = pl.BlockSpec(memory_space=pltpu.VMEM)
    far = pl.BlockSpec(memory_space=pl.ANY)
    return pl.pallas_call(
        functools.partial(wave_kernel, n_tx, n_ty),
        out_shape=(
            jax.ShapeDtypeStruct(wave_now.shape, jnp.float32),
            jax.ShapeDtypeStruct(wave_now.shape, jnp.float32),
            jax.ShapeDtypeStruct((STEPS, shots, points), jnp.float32),
        ),
        in_specs=[far, far, whole, whole],
        out_specs=(far, far, whole),
        scratch_shapes=[
            pltpu.VMEM((STEPS + 2, shots, ext_x + 2, ext_y, depth), jnp.float32),
            pltpu.VMEM((STEPS + 1, 2, shots, ext_x, 1, depth), jnp.float32),
            pltpu.VMEM((STEPS + 1, 2, shots, ext_x, 1, depth), jnp.float32),
            pltpu.VMEM((ext_x * ext_y, points), jnp.bfloat16),
            pltpu.VMEM((depth, points), jnp.float32),
            pltpu.SemaphoreType.DMA((2,)),
            pltpu.SemaphoreType.DMA((STEPS + 1, 4)),
            pltpu.SemaphoreType.DMA((STEPS + 1, 4)),
        ],
        compiler_params=pltpu.CompilerParams(
            collective_id=0, has_side_effects=True, vmem_limit_bytes=40 * MIB
        ),
    )(wave_now, wave_prev, courant, ridx)


def inject_kernel(wave_ref, cells_ref, weights_ref, last_ref, out_ref):
    shots, ext_x, ext_y, depth = wave_ref.shape
    corners, points = cells_ref.shape
    rows = lax.broadcasted_iota(jnp.int32, (ext_x * ext_y, points), 0)
    deep = lax.broadcasted_iota(jnp.int32, (depth, points), 0)
    totals = [wave_ref[s].reshape(ext_x * ext_y, depth) for s in range(shots)]
    for k in range(corners):
        cells = cells_ref[k : k + 1, :]
        pick = jnp.where(rows == cells // depth, 1.0, 0.0).astype(jnp.bfloat16)
        here = deep == cells % depth
        values = weights_ref[k : k + 1, :] * last_ref[...]
        for s in range(shots):
            spread = jnp.where(here, values[s : s + 1, :], 0.0).astype(jnp.bfloat16)
            totals[s] += lax.dot_general(
                pick, spread, (((1,), (1,)), ((), ())), preferred_element_type=jnp.float32
            )
    for s in range(shots):
        out_ref[s] = totals[s].reshape(ext_x, ext_y, depth)


def inject(wave, cells, weights, last):
    whole = pl.BlockSpec(memory_space=pltpu.VMEM)
    return pl.pallas_call(
        inject_kernel,
        out_shape=jax.ShapeDtypeStruct(wave.shape, jnp.float32),
        in_specs=[whole] * 4,
        out_specs=whole,
        compiler_params=pltpu.CompilerParams(vmem_limit_bytes=40 * MIB),
    )(wave, cells, weights, last)


def local(
    n_tx, n_ty,
    wave_now, wave_prev, courant, rec_index, rec_history, green, lag_delay, emit_cells, emit_weights
):
    shots_here = wave_now.shape[0]
    previous, current, records = run_wave(
        n_tx, n_ty, wave_now, wave_prev, courant, rec_index.reshape(1, -1)
    )
    history_here = rec_history.reshape(shots_here, HIST, -1)
    new_here = records.astype(jnp.bfloat16).transpose(1, 0, 2)
    full_here = jnp.concatenate([history_here, new_here], 1)
    piece = lax.all_gather(full_here, "shot", axis=0, tiled=True)
    total = jnp.zeros((piece.shape[0], STEPS, green.shape[2]), jnp.float32)
    for lag_group in range(green.shape[0]):
        offset = HIST - lag_delay[lag_group]
        window = lax.dynamic_slice_in_dim(piece, offset, STEPS, 1)
        total = total + jnp.einsum(
            "str,rq->stq", window, green[lag_group], preferred_element_type=jnp.float32
        )
    summed = lax.psum_scatter(total, ("tx", "ty"), scatter_dimension=2, tiled=True)
    owned = lax.all_to_all(summed, "shot", split_axis=0, concat_axis=2, tiled=True)
    last = owned[:, STEPS - 1, :]
    wave_out = inject(
        current,
        emit_cells.reshape(emit_cells.shape[-2:]),
        emit_weights.reshape(emit_weights.shape[-2:]),
        last,
    )
    emission = owned.reshape(shots_here, STEPS, 1, 1, -1)
    return (wave_out, previous, emission)


def solution(mesh):
    return jax.shard_map(
        functools.partial(local, mesh.shape["tx"], mesh.shape["ty"]),
        mesh=mesh,
        in_specs=(
            P("shot", "tx", "ty", None),
            P("shot", "tx", "ty", None),
            P("tx", "ty", None),
            P("tx", "ty", None),
            P("shot", None, "tx", "ty", None),
            P(None, ("tx", "ty"), "shot"),
            P(),
            P("tx", "ty", None, None),
            P("tx", "ty", None, None),
        ),
        out_specs=(
            P("shot", "tx", "ty", None),
            P("shot", "tx", "ty", None),
            P("shot", None, "tx", "ty", None),
        ),
        check_vma=False,
    )
```

profile of v0, /device:TPU:0, one launch (start us, length us, event | category | flops | bytes accessed | tf_op | source)
XLA Modules:
  0.0 137.2 jit_solution(4357644465700874279)
XLA Ops:
  7.2 0.0 reduce-scatter.2.cloned.1.call-start
  7.2 1.3 fusion.9
  11.1 0.8 copy.27
  11.9 0.0 copy-start
  11.9 1.0 copy-done
  12.9 0.0 copy-start.1
  12.9 1.0 copy-done.1
  14.0 0.0 copy-start.2
  14.0 0.9 copy-done.2
  14.9 0.0 copy-start.5
  14.9 0.7 copy-done.5
  15.6 33.7 %shard_map.112 = (f32[4,16,16,128]{3,2,1,0:T(8,128)S(1)}, f32[4,16,16,128]{3,2,1,0:T(8,128)S(1)}, f32[8,4,512]{2,1,0:T(4,128)S(1)}) custom-call(f32[4,16,16,128]{3,2,1,0:T(8,128)S(1)} %copy-done, f32[4,16,16,128]{3,2,1,0:T(8,128)S(1)} %copy-done.1, f32[16,16,128]{2,1,0:T(8,128)S(1)} %copy-done.2, s32[1,512]{1,0:T(1,128)S(1)} %bitcast.33), custom_call_target="tpu_custom_call" | custom-call | tf_op jit(solution)/shard_map/pallas_call | solution.py:173
  49.4 4.9 %all_gather.3 = bf16[8,16,512]{2,1,0:T(8,128)(2,1)S(1)} all-gather(bf16[4,16,512]{2,1,0:T(8,128)(2,1)S(1)} %copy.18), channel_id=1, replica_groups=mesh['shot'=2,'tx'=4,'ty'=4] {'shot'}, dimensions={0}, use_global_device_ids=true | all-gather | bytes 196608 | tf_op jit(solution)/shard_map/all_gather | solution.py:240
  54.3 0.0 copy-start.3
  54.3 0.0 copy-start.4
  54.3 3.0 %fusion.1 = f32[8,8,4096]{2,1,0:T(8,128)S(1)} fusion(bf16[2,512,4096]{2,1,0:T(8,128)(2,1)} %param.14, bf16[8,16,512]{2,1,0:T(8,128)(2,1)S(1)} %all_gather.3, s32[]{:T(128)S(6)} %select_n.6), kind=kOutput, calls=%fused_computation.2 | convolution fusion | flops 268435456 | bytes 5308420 | tf_op jit(solution)/shard_map/str,rq->stq/dot_general | solution.py:245
  57.4 4.0 %convolution_add_fusion = f32[8,8,4096]{2,1,0:T(8,128)} fusion(f32[8,8,4096]{2,1,0:T(8,128)S(1)} %fusion.1, bf16[2,512,4096]{2,1,0:T(8,128)(2,1)} %param.14, bf16[8,16,512]{2,1,0:T(8,128)(2,1)S(1)} %all_gather.3, s32[]{:T(128)S(6)} %select_n.7), kind=kOutput, calls=%fused_computation | convolution fusion | flops 268697600 | bytes 6356996 | tf_op jit(solution)/shard_map/str,rq->stq/dot_general | solution.py:245
  61.4 0.0 reduce-scatter.2.cloned.1.call-update
  61.4 56.7 %reduce-scatter.2.cloned.1.call-done = f32[8,8,256]{2,1,0:T(8,128)} async-done(((f32[8,8,4096]{2,1,0:T(8,128)}), f32[8,8,256]{2,1,0:T(8,128)}) %reduce-scatter.2.cloned.1.call-update) | async-done | bytes 65552 | tf_op jit(solution)/shard_map/reduce_scatter | solution.py:248
  118.1 3.3 %all-to-all-start = ((f32[8,8,256]{2,1,0:T(8,128)}), f32[8,8,256]{2,1,0:T(8,128)S(1)}, u32[]{:S(2)}, u32[]{:S(2)}) async-start(f32[8,8,256]{2,1,0:T(8,128)} %reduce-scatter.2.cloned.1.call-done), calls=%async_computation.1 | async-start | bytes 131072 | tf_op jit(solution)/shard_map/all_to_all | solution.py:249
  121.4 4.1 %all-to-all-done = f32[8,8,256]{2,1,0:T(8,128)S(1)} async-done(((f32[8,8,256]{2,1,0:T(8,128)}), f32[8,8,256]{2,1,0:T(8,128)S(1)}, u32[]{:S(2)}, u32[]{:S(2)}) %all-to-all-start) | async-done | bytes 65568 | tf_op jit(solution)/shard_map/all_to_all | solution.py:249
  125.5 0.1 copy.25
  125.6 0.1 copy.26
  125.6 0.1 all_to_all.16
  125.7 0.7 reshape.34
  126.5 0.0 copy-done.3
  126.5 0.0 copy-done.4
  126.5 3.2 %shard_map.113 = f32[4,16,16,128]{3,2,1,0:T(8,128)} custom-call(f32[4,16,16,128]{3,2,1,0:T(8,128)S(1)} %get-tuple-element.6.wave_ref, s32[8,512]{1,0:T(8,128)S(1)} %bitcast.31, f32[8,512]{1,0:T(8,128)S(1)} %bitcast.32, f32[4,512]{1,0:T(4,128)S(1)} %slice_bitcast_fusion.last_ref), custom_call_target="tpu_custom_call" | custom-call | tf_op jit(solution)/shard_map/pallas_call | solution.py:220
  129.6 0.8 copy.29
  (4 shorter events, 0.1 us)
Async XLA Ops:
  7.2 111.0 %reduce-scatter.2.cloned.1.call-start = ((), (), s32[]{:S(2)}) async-start(), calls=%async_computation.2 | async-start | bytes 1114112 | tf_op jit(solution)/shard_map/reduce_scatter | solution.py:248
  11.9 1.0 copy-start
  12.9 1.0 copy-start.1
  14.0 0.9 copy-start.2
  14.9 0.7 copy-start.5
  54.3 72.1 %copy-start.3 = (s32[1,1,8,512]{3,2,1,0:T(8,128)S(1)}, s32[1,1,8,512]{3,2,1,0:T(8,128)}, u32[]{:S(2)}) copy-start(s32[1,1,8,512]{3,2,1,0:T(8,128)} %param.16) | copy-start | bytes 49156
  54.3 72.1 %copy-start.4 = (f32[1,1,8,512]{3,2,1,0:T(8,128)S(1)}, f32[1,1,8,512]{3,2,1,0:T(8,128)}, u32[]{:S(2)}) copy-start(f32[1,1,8,512]{3,2,1,0:T(8,128)} %param.17) | copy-start | bytes 49156
  118.1 7.4 %all-to-all-start = ((f32[8,8,256]{2,1,0:T(8,128)}), f32[8,8,256]{2,1,0:T(8,128)S(1)}, u32[]{:S(2)}, u32[]{:S(2)}) async-start(f32[8,8,256]{2,1,0:T(8,128)} %reduce-scatter.2.cloned.1.call-done), calls=%async_computation.1 | async-start | bytes 131072 | tf_op jit(solution)/shard_map/all_to_all | solution.py:249
Sparse Core Ops, SparseCore 0:
  61.6 56.5 reduce-scatter.1
where the time goes:
time: 138 us; the launch traced here: 137 us
  waiting for transfers between devices  60.8 us (44%)
  Pallas kernels  36.8 us (27%)
  between operations  16.7 us (12%)
  local copies, waits for them, and re-layouts  7.47 us (5%)
  matrix products  7.09 us (5%)
  blocking collectives  4.94 us (4%)
  starting transfers between devices  3.33 us (2%)
    reduce_scatter x1, waiting for transfers between devices, local(): lax.psum_scatter(total, ('tx', 'ty'), scatter_dimension=2, tiled=True)  56.7 us
    pallas_call x1, Pallas kernels, run_wave(): pl.pallas_call(functools.partial(wave_kernel, n_tx, n_ty), out_shape=(jax...  33.7 us
    dot_general x2, matrix products, local(): jnp.einsum('str,rq->stq', window, green[lag_group], preferred_element_typ...  7.09 us
    unnamed x14, local copies, waits for them, and re-layouts  5.24 us
    all_gather x1, blocking collectives, local(): piece = lax.all_gather(full_here, 'shot', axis=0, tiled=True)  4.94 us
    all_to_all x1, waiting for transfers between devices, local(): lax.all_to_all(summed, 'shot', split_axis=0, concat_axis=2, tiled=True)  4.11 us
    all_to_all x1, starting transfers between devices, local(): lax.all_to_all(summed, 'shot', split_axis=0, concat_axis=2, tiled=True)  3.29 us
    pallas_call x1, Pallas kernels, inject(): pl.pallas_call(inject_kernel, out_shape=jax.ShapeDtypeStruct(wave.shape,...  3.15 us
  transfers between devices with their start and end apart: 2, of which 2 were waited for; matrix products, arithmetic and copies ran while one was open for 0% of the time, Pallas kernels for 0%

commit v1 on v0

--- a/solution.py
+++ b/solution.py
@@ -12,14 +12,53 @@
 MIB = 1024 * 1024
 
 
-def wave_kernel(
-    n_tx, n_ty, now_ref, prev_ref, cour_ref, ridx_ref,
-    last_ref, out_ref, rec_ref,
+def flip(index, bit):
+    return index + bit * (1 - 2 * ((index // bit) % 2))
+
+
+def low_bit(m):
+    return m & -m
+
+
+def block_kernel(
+    n_shot, n_tx, n_ty, lag_ref, now_ref, prev_ref, cour_ref, ridx_ref, hist_ref, green_ref,
+    last_ref, out_ref, em_ref,
     field, ysend, yrecv, pick_xy, pick_z,
-    load_sem, send_sem, recv_sem,
+    hist_all, rec, rec_all, early, blocks, xpart, xrecv, zpart, zsend, zrecv,
+    load_sem, send_sem, recv_sem, green_sem, hist_send, hist_recv, rec_send, rec_recv,
+    x_send, x_recv, z_send, z_recv,
 ):
+    mesh_id = pl.DeviceIdType.MESH
     shots, ext_x, ext_y, depth = now_ref.shape
     tx, ty = lax.axis_index("tx"), lax.axis_index("ty")
+    me = lax.axis_index("shot")
+    span = early.shape[2]
+    each = span // n_ty
+    rows_each = hist_ref.shape[0]
+    group_a = jnp.where(lag_ref[0] == HIST, 0, 1)
+    group_b = 1 - group_a
+    short = jnp.where(lag_ref[0] == HIST, lag_ref[1], lag_ref[0])
+
+    def green_tile(m):
+        tile = tx
+        bit = 1
+        while bit < n_tx:
+            if m & bit:
+                tile = flip(tile, bit)
+            bit *= 2
+        return tile
+
+    green_loads = []
+    for group in range(green_ref.shape[0]):
+        for m in range(n_tx):
+            if span % 128 == 0:
+                start = pl.multiple_of(green_tile(m) * span, span)
+                src = green_ref.at[group, :, pl.ds(start, span)]
+            else:
+                src = green_ref.at[group, green_tile(m)]
+            green_loads.append(
+                pltpu.make_async_copy(src, blocks.at[group, m], green_sem.at[group, m])
+            )
     there = (tx > 0, tx < n_tx - 1, ty > 0, ty < n_ty - 1)
     target = ({"tx": tx - 1}, {"tx": tx + 1}, {"ty": ty - 1}, {"ty": ty + 1})
 
@@ -27,16 +66,36 @@
         pltpu.make_async_copy(prev_ref, field.at[0, :, pl.ds(1, ext_x)], load_sem.at[0]),
         pltpu.make_async_copy(now_ref, field.at[1, :, pl.ds(1, ext_x)], load_sem.at[1]),
     ]
-    for load in loads:
+    for load in loads + green_loads:
         load.start()
 
     barrier = pltpu.get_barrier_semaphore()
-    for side in range(4):
-        @pl.when(there[side])
-        def _():
-            pl.semaphore_signal(
-                barrier, inc=1, device_id=target[side], device_id_type=pl.DeviceIdType.MESH
-            )
+    offsets = [
+        (far, di) for far in range(n_ty) for di in range(n_shot) if far or di
+    ]
+    for step_x in range(1, n_tx):
+        pl.semaphore_signal(
+            barrier, inc=1, device_id={"tx": (tx + step_x) % n_tx}, device_id_type=mesh_id
+        )
+
+    def place(far, di):
+        return (me + di) % n_shot, (ty + far) % n_ty
+
+    for far, di in offsets:
+        shot_to, ty_to = place(far, di)
+        pl.semaphore_signal(
+            barrier, inc=1, device_id={"shot": shot_to, "ty": ty_to}, device_id_type=mesh_id
+        )
+
+    def share(store, sends, recvs, di):
+        return pltpu.make_async_remote_copy(
+            src_ref=store.at[0], dst_ref=store.at[di],
+            send_sem=sends.at[di], recv_sem=recvs.at[di],
+            device_id={"shot": (me + di) % n_shot}, device_id_type=mesh_id,
+        )
+
+    hist_all[0] = hist_ref[...]
+    rec[...] = jnp.zeros(rec.shape, jnp.float32)
 
     for side in range(4):
         @pl.when(jnp.logical_not(there[side]))
@@ -94,9 +153,10 @@
 
     for load in loads:
         load.wait()
-    peers = sum(jnp.where(flag, 1, 0) for flag in there)
-    pl.semaphore_wait(barrier, peers)
+    pl.semaphore_wait(barrier, n_tx - 1 + len(offsets))
     send(1)
+    for di in range(1, n_shot):
+        share(hist_all, hist_send, hist_recv, di).start()
 
     part = 4 if ext_x % 4 == 0 else 1
     shape = (part, ext_y, depth)
@@ -128,7 +188,9 @@
             found = lax.dot_general(
                 tile, pick_xy[...], (((0,), (0,)), ((), ())), preferred_element_type=jnp.float32
             )
-            rec_ref[slot - 2, s : s + 1, :] = jnp.sum(found * pick_z[...], axis=0, keepdims=True)
+            rec[pl.ds(s * STEPS + slot - 2, 1), :] = jnp.sum(
+                found * pick_z[...], axis=0, keepdims=True
+            )
 
     def arrive(slot):
         for side in range(4):
@@ -136,23 +198,99 @@
             def _():
                 landing(slot, side).wait_recv()
 
+    first_early = 2
+
+    def early_part(m):
+        early[m] = jnp.dot(
+            hist_all[...].reshape(n_shot * rows_each, points), blocks[group_a, m],
+            preferred_element_type=jnp.float32,
+        )
+
     def step(slot, carry):
         arrive(slot)
         advance(slot)
         send(slot + 1)
         sample(slot + 1)
+
+        @pl.when(slot == first_early)
+        def _():
+            for load in green_loads:
+                load.wait()
+            for di in range(1, n_shot):
+                share(hist_all, hist_send, hist_recv, di).wait()
+
+        @pl.when(jnp.logical_and(slot >= first_early, slot < first_early + n_tx))
+        def _():
+            early_part(slot - first_early)
         return carry
 
     lax.fori_loop(1, STEPS, step, 0)
+    for m in range(STEPS - first_early, n_tx):
+        early_part(m)
+
+    rec_all[0] = rec[...].astype(jnp.bfloat16)
+    for di in range(1, n_shot):
+        share(rec_all, rec_send, rec_recv, di).start()
     arrive(STEPS)
     advance(STEPS)
-    sample(STEPS + 1)
     stores = [
         pltpu.make_async_copy(field.at[STEPS, :, pl.ds(1, ext_x)], last_ref, load_sem.at[0]),
         pltpu.make_async_copy(field.at[STEPS + 1, :, pl.ds(1, ext_x)], out_ref, load_sem.at[1]),
     ]
     for store in stores:
         store.start()
+    for di in range(1, n_shot):
+        share(rec_all, rec_send, rec_recv, di).wait()
+
+    to_row = lax.broadcasted_iota(jnp.int32, (rows_each, rows_each), 0)
+    of_row = lax.broadcasted_iota(jnp.int32, (rows_each, rows_each), 1)
+    same = to_row // STEPS == of_row // STEPS
+    wanted = to_row % STEPS - short
+    pick_old = jnp.where(same & (of_row % STEPS == wanted + HIST), 1.0, 0.0).astype(jnp.bfloat16)
+    pick_new = jnp.where(same & (of_row % STEPS == wanted), 1.0, 0.0).astype(jnp.bfloat16)
+    windows = []
+    for di in range(n_shot):
+        window = jnp.dot(pick_old, hist_all[di], preferred_element_type=jnp.float32)
+        window += jnp.dot(pick_new, rec_all[di], preferred_element_type=jnp.float32)
+        windows.append(window.astype(jnp.bfloat16))
+    window = jnp.concatenate(windows, 0)
+
+    def hand_on(m):
+        bit = low_bit(m)
+        return pltpu.make_async_remote_copy(
+            src_ref=xpart.at[m], dst_ref=xrecv.at[m],
+            send_sem=x_send.at[m], recv_sem=x_recv.at[m],
+            device_id={"tx": flip(tx, bit)}, device_id_type=mesh_id,
+        )
+
+    for m in range(n_tx - 1, -1, -1):
+        part = early[m] + jnp.dot(window, blocks[group_b, m], preferred_element_type=jnp.float32)
+        for di in range(n_shot):
+            xpart[m, (me - di + n_shot) % n_shot] = part[di * rows_each : (di + 1) * rows_each]
+        bit = 1
+        while bit < (low_bit(m) if m else n_tx):
+            hand_on(m + bit).wait_recv()
+            xpart[m] += xrecv[m + bit]
+            bit *= 2
+        if m:
+            hand_on(m).start()
+
+    for b in range(n_ty):
+        for i in range(n_shot):
+            tile = xpart[0, i, :, b * each : (b + 1) * each]
+            zpart[b, i] = tile
+            zsend[b, i] = tile.astype(jnp.bfloat16)
+
+    def deliver(far, di):
+        shot_to, ty_to = place(far, di)
+        return pltpu.make_async_remote_copy(
+            src_ref=zsend.at[ty_to, shot_to], dst_ref=zrecv.at[far, di],
+            send_sem=z_send.at[far, di], recv_sem=z_recv.at[far, di],
+            device_id={"shot": shot_to, "ty": ty_to}, device_id_type=mesh_id,
+        )
+
+    for far, di in reversed(offsets):
+        deliver(far, di).start()
 
     def drain(slot, carry):
         for side in range(4):
@@ -161,23 +299,45 @@
                 copy(slot, side).wait_send()
         return carry
     lax.fori_loop(1, STEPS + 1, drain, 0)
+    for m in range(1, n_tx):
+        hand_on(m).wait_send()
+
+    for di in range(n_shot):
+        if di == 0:
+            total = zpart[ty, me]
+        else:
+            deliver(0, di).wait()
+            total = zrecv[0, di].astype(jnp.float32)
+        for far in range(1, n_ty):
+            deliver(far, di).wait()
+            total += zrecv[far, di].astype(jnp.float32)
+        em_ref[(me - di + n_shot) % n_shot] = total
     for store in stores:
         store.wait()
 
 
-def run_wave(n_tx, n_ty, wave_now, wave_prev, courant, ridx):
+def run_block(n_shot, n_tx, n_ty, lag_delay, wave_now, wave_prev, courant, ridx, history, green):
     shots, ext_x, ext_y, depth = wave_now.shape
     points = ridx.shape[1]
+    groups = green.shape[0]
+    rows_each = history.shape[0]
+    span = green.shape[2] // n_tx
+    each = span // n_ty
+    if span % 128:
+        green = green.reshape(groups, points, n_tx, span).transpose(0, 2, 1, 3)
     whole = pl.BlockSpec(memory_space=pltpu.VMEM)
     far = pl.BlockSpec(memory_space=pl.ANY)
+    dma = pltpu.SemaphoreType.DMA
     return pl.pallas_call(
-        functools.partial(wave_kernel, n_tx, n_ty),
+        functools.partial(block_kernel, n_shot, n_tx, n_ty),
         out_shape=(
             jax.ShapeDtypeStruct(wave_now.shape, jnp.float32),
             jax.ShapeDtypeStruct(wave_now.shape, jnp.float32),
-            jax.ShapeDtypeStruct((STEPS, shots, points), jnp.float32),
+            jax.ShapeDtypeStruct((n_shot, rows_each, each), jnp.float32),
         ),
-        in_specs=[far, far, whole, whole],
+        in_specs=[
+            pl.BlockSpec(memory_space=pltpu.SMEM), far, far, whole, whole, whole, far
+        ],
         out_specs=(far, far, whole),
         scratch_shapes=[
             pltpu.VMEM((STEPS + 2, shots, ext_x + 2, ext_y, depth), jnp.float32),
@@ -185,14 +345,33 @@
             pltpu.VMEM((STEPS + 1, 2, shots, ext_x, 1, depth), jnp.float32),
             pltpu.VMEM((ext_x * ext_y, points), jnp.bfloat16),
             pltpu.VMEM((depth, points), jnp.float32),
-            pltpu.SemaphoreType.DMA((2,)),
-            pltpu.SemaphoreType.DMA((STEPS + 1, 4)),
-            pltpu.SemaphoreType.DMA((STEPS + 1, 4)),
+            pltpu.VMEM((n_shot, rows_each, points), jnp.bfloat16),
+            pltpu.VMEM((rows_each, points), jnp.float32),
+            pltpu.VMEM((n_shot, rows_each, points), jnp.bfloat16),
+            pltpu.VMEM((n_tx, n_shot * rows_each, span), jnp.float32),
+            pltpu.VMEM((groups, n_tx, points, span), jnp.bfloat16),
+            pltpu.VMEM((n_tx, n_shot, rows_each, span), jnp.float32),
+            pltpu.VMEM((n_tx, n_shot, rows_each, span), jnp.float32),
+            pltpu.VMEM((n_ty, n_shot, rows_each, each), jnp.float32),
+            pltpu.VMEM((n_ty, n_shot, rows_each, each), jnp.bfloat16),
+            pltpu.VMEM((n_ty, n_shot, rows_each, each), jnp.bfloat16),
+            dma((2,)),
+            dma((STEPS + 1, 4)),
+            dma((STEPS + 1, 4)),
+            dma((groups, n_tx)),
+            dma((n_shot,)),
+            dma((n_shot,)),
+            dma((n_shot,)),
+            dma((n_shot,)),
+            dma((n_tx,)),
+            dma((n_tx,)),
+            dma((n_ty, n_shot)),
+            dma((n_ty, n_shot)),
         ],
         compiler_params=pltpu.CompilerParams(
-            collective_id=0, has_side_effects=True, vmem_limit_bytes=40 * MIB
+            collective_id=0, has_side_effects=True, vmem_limit_bytes=52 * MIB
         ),
-    )(wave_now, wave_prev, courant, ridx)
+    )(lag_delay, wave_now, wave_prev, courant, ridx, history, green)
 
 
 def inject_kernel(wave_ref, cells_ref, weights_ref, last_ref, out_ref):
@@ -227,40 +406,28 @@
 
 
 def local(
-    n_tx, n_ty,
+    n_shot, n_tx, n_ty,
     wave_now, wave_prev, courant, rec_index, rec_history, green, lag_delay, emit_cells, emit_weights
 ):
     shots_here = wave_now.shape[0]
-    previous, current, records = run_wave(
-        n_tx, n_ty, wave_now, wave_prev, courant, rec_index.reshape(1, -1)
+    previous, current, columns = run_block(
+        n_shot, n_tx, n_ty, lag_delay, wave_now, wave_prev, courant,
+        rec_index.reshape(1, -1), rec_history.reshape(shots_here * HIST, -1), green,
     )
-    history_here = rec_history.reshape(shots_here, HIST, -1)
-    new_here = records.astype(jnp.bfloat16).transpose(1, 0, 2)
-    full_here = jnp.concatenate([history_here, new_here], 1)
-    piece = lax.all_gather(full_here, "shot", axis=0, tiled=True)
-    total = jnp.zeros((piece.shape[0], STEPS, green.shape[2]), jnp.float32)
-    for lag_group in range(green.shape[0]):
-        offset = HIST - lag_delay[lag_group]
-        window = lax.dynamic_slice_in_dim(piece, offset, STEPS, 1)
-        total = total + jnp.einsum(
-            "str,rq->stq", window, green[lag_group], preferred_element_type=jnp.float32
-        )
-    summed = lax.psum_scatter(total, ("tx", "ty"), scatter_dimension=2, tiled=True)
-    owned = lax.all_to_all(summed, "shot", split_axis=0, concat_axis=2, tiled=True)
-    last = owned[:, STEPS - 1, :]
+    owned = columns.reshape(n_shot, shots_here, STEPS, -1).transpose(1, 2, 0, 3)
+    owned = owned.reshape(shots_here, STEPS, -1)
     wave_out = inject(
         current,
         emit_cells.reshape(emit_cells.shape[-2:]),
         emit_weights.reshape(emit_weights.shape[-2:]),
-        last,
+        owned[:, STEPS - 1, :],
     )
-    emission = owned.reshape(shots_here, STEPS, 1, 1, -1)
-    return (wave_out, previous, emission)
+    return (wave_out, previous, owned.reshape(shots_here, STEPS, 1, 1, -1))
 
 
 def solution(mesh):
     return jax.shard_map(
-        functools.partial(local, mesh.shape["tx"], mesh.shape["ty"]),
+        functools.partial(local, mesh.shape["shot"], mesh.shape["tx"], mesh.shape["ty"]),
         mesh=mesh,
         in_specs=(
             P("shot", "tx", "ty", None),

time: 138 us -> 60.4 us (0.44)
  waiting for transfers between devices: 60.8 us -> 0 us
  Pallas kernels: 36.8 us -> 53.7 us
  between operations: 16.7 us -> 0.7 us
  matrix products: 7.09 us -> 0 us
  blocking collectives: 4.94 us -> 0 us
  starting transfers between devices: 3.33 us -> 0 us
  local copies, waits for them, and re-layouts: 7.47 us -> 5.73 us
    reduce_scatter x1 -> x0, waiting for transfers between devices: 56.7 us -> none  [local(): lax.psum_scatter(total, ('tx', 'ty'), scatter_dimension=2, tiled=True)]
    pallas_call x1, Pallas kernels: 33.7 us -> 50.6 us  [run_block(): pl.pallas_call(functools.partial(block_kernel, n_shot, n_tx, n_ty), out_s...]
    dot_general x2 -> x0, matrix products: 7.09 us -> none  [local(): jnp.einsum('str,rq->stq', window, green[lag_group], preferred_element_typ...]
    all_gather x1 -> x0, blocking collectives: 4.94 us -> none  [local(): piece = lax.all_gather(full_here, 'shot', axis=0, tiled=True)]
    all_to_all x1 -> x0, waiting for transfers between devices: 4.11 us -> none  [local(): lax.all_to_all(summed, 'shot', split_axis=0, concat_axis=2, tiled=True)]
    all_to_all x1 -> x0, starting transfers between devices: 3.29 us -> none  [local(): lax.all_to_all(summed, 'shot', split_axis=0, concat_axis=2, tiled=True)]
    unnamed x14 -> x15, local copies, waits for them, and re-layouts: 5.24 us -> 4.83 us
  transfers between devices with their start and end apart: 2 -> 0, of which waited for: 2 -> 0; matrix products, arithmetic and copies ran while one was open for 0% -> 0% of each run, Pallas kernels for 0% -> 0%
where the time goes in v1:
time: 60.4 us; the launch traced here: 60.2 us
  Pallas kernels  53.7 us (89%)
  local copies, waits for them, and re-layouts  5.73 us (9%)
  between operations  0.7 us (1%)
    pallas_call x1, Pallas kernels, run_block(): pl.pallas_call(functools.partial(block_kernel, n_shot, n_tx, n_ty), out_s...  50.6 us
    unnamed x15, local copies, waits for them, and re-layouts  4.83 us
    pallas_call x1, Pallas kernels, inject(): pl.pallas_call(inject_kernel, out_shape=jax.ShapeDtypeStruct(wave.shape,...  3.15 us

profile of v1, /device:TPU:0, one launch (start us, length us, event | category | flops | bytes accessed | tf_op | source)
XLA Modules:
  0.0 60.2 jit_solution(6579318500271901787)
XLA Ops:
  0.6 0.0 copy-start
  0.6 1.0 %copy-done = f32[4,16,16,128]{3,2,1,0:T(8,128)S(1)} copy-done((f32[4,16,16,128]{3,2,1,0:T(8,128)S(1)}, f32[4,16,16,128]{3,2,1,0:T(8,128)}, u32[]{:S(2)}) %copy-start) | copy-done | bytes 524312
  1.7 0.0 copy-start.1
  1.7 0.9 %copy-done.1 = f32[16,16,128]{2,1,0:T(8,128)S(1)} copy-done((f32[16,16,128]{2,1,0:T(8,128)S(1)}, f32[16,16,128]{2,1,0:T(8,128)}, u32[]{:S(2)}) %copy-start.1) | copy-done | bytes 131096
  2.6 0.0 copy-start.2
  2.6 0.8 %copy-done.2 = bf16[4,8,1,1,512]{4,1,3,2,0:T(8,128)(2,1)S(1)} copy-done((bf16[4,8,1,1,512]{4,1,3,2,0:T(8,128)(2,1)S(1)}, bf16[4,8,1,1,512]{4,1,3,2,0:T(8,128)(2,1)}, u32[]{:S(2)}) %copy-start.2) | copy-done | bytes 32792
  3.3 0.0 copy-start.5
  3.3 0.7 %copy-done.5 = s32[1,1,512]{2,1,0:T(1,128)S(1)} copy-done((s32[1,1,512]{2,1,0:T(1,128)S(1)}, s32[1,1,512]{2,1,0:T(1,128)}, u32[]{:S(2)}) %copy-start.5) | copy-done | bytes 2072
  4.0 0.0 copy-start.6
  4.0 0.7 %copy-done.6 = s32[2]{0:T(128)S(1)} copy-done((s32[2]{0:T(128)S(1)}, s32[2]{0:T(128)}, u32[]{:S(2)}) %copy-start.6) | copy-done | bytes 32
  4.7 0.0 copy-start.3
  4.7 0.0 copy-start.4
  4.7 50.6 %shard_map.112 = (f32[4,16,16,128]{3,2,1,0:T(8,128)S(1)}, f32[4,16,16,128]{3,2,1,0:T(8,128)S(1)}, f32[2,32,256]{2,1,0:T(8,128)S(1)}) custom-call(s32[2]{0:T(128)S(1)} %copy-done.6, f32[4,16,16,128]{3,2,1,0:T(8,128)S(1)} %copy-done, f32[4,16,16,128]{3,2,1,0:T(8,128)} %prev_ref.1, f32[16,16,128]{2,1,0:T(8,128)S(1)} %copy-done.1, s32[1,512]{1,0:T(1,128)S(1)} %bitcast.20, ...), custom_call_target="tpu_custom_call" | custom-call | tf_op jit(solution)/shard_map/pallas_call | solution.py:331
  55.3 0.1 copy.17
  55.3 0.1 copy.18
  55.4 0.1 reshape.29
  55.5 0.0 copy-done.3
  55.5 0.0 copy-done.4
  55.5 3.2 %shard_map.113 = f32[4,16,16,128]{3,2,1,0:T(8,128)} custom-call(f32[4,16,16,128]{3,2,1,0:T(8,128)S(1)} %get-tuple-element.6.wave_ref, s32[8,512]{1,0:T(8,128)S(1)} %bitcast.18, f32[8,512]{1,0:T(8,128)S(1)} %bitcast.19, f32[4,512]{1,0:T(4,128)S(1)} %slice_bitcast_fusion.last_ref), custom_call_target="tpu_custom_call" | custom-call | tf_op jit(solution)/shard_map/pallas_call | solution.py:399
  58.6 0.7 %reshape_reshape.3 = f32[4,8,1,1,512]{4,3,2,1,0:T(1,128)} reshape(f32[4,8,2,256]{3,2,1,0:T(2,128)S(1)} %bitcast.21) | data formatting | bytes 131072 | tf_op jit(solution)/shard_map/reshape;reshape | solution.py:425
  59.4 0.8 %copy.20 = f32[4,16,16,128]{3,2,1,0:T(8,128)} copy(f32[4,16,16,128]{3,2,1,0:T(8,128)S(1)} %get-tuple-element.13) | data formatting | bytes 1048576
  (1 shorter events, 0.0 us)
Async XLA Ops:
  0.6 1.0 %copy-start = (f32[4,16,16,128]{3,2,1,0:T(8,128)S(1)}, f32[4,16,16,128]{3,2,1,0:T(8,128)}, u32[]{:S(2)}) copy-start(f32[4,16,16,128]{3,2,1,0:T(8,128)} %now_ref.1) | copy-start | bytes 1572868
  1.7 0.9 %copy-start.1 = (f32[16,16,128]{2,1,0:T(8,128)S(1)}, f32[16,16,128]{2,1,0:T(8,128)}, u32[]{:S(2)}) copy-start(f32[16,16,128]{2,1,0:T(8,128)} %cour_ref.1) | copy-start | bytes 393220
  2.6 0.8 %copy-start.2 = (bf16[4,8,1,1,512]{4,1,3,2,0:T(8,128)(2,1)S(1)}, bf16[4,8,1,1,512]{4,1,3,2,0:T(8,128)(2,1)}, u32[]{:S(2)}) copy-start(bf16[4,8,1,1,512]{4,1,3,2,0:T(8,128)(2,1)} %param.13) | copy-start | bytes 98308
  3.3 0.7 %copy-start.5 = (s32[1,1,512]{2,1,0:T(1,128)S(1)}, s32[1,1,512]{2,1,0:T(1,128)}, u32[]{:S(2)}) copy-start(s32[1,1,512]{2,1,0:T(1,128)} %param.12) | copy-start | bytes 6148
  4.0 0.7 %copy-start.6 = (s32[2]{0:T(128)S(1)}, s32[2]{0:T(128)}, u32[]{:S(2)}) copy-start(s32[2]{0:T(128)} %lag_ref.1) | copy-start | bytes 28
  4.7 50.8 %copy-start.3 = (s32[1,1,8,512]{3,2,1,0:T(8,128)S(1)}, s32[1,1,8,512]{3,2,1,0:T(8,128)}, u32[]{:S(2)}) copy-start(s32[1,1,8,512]{3,2,1,0:T(8,128)} %param.16) | copy-start | bytes 49156
  4.7 50.8 %copy-start.4 = (f32[1,1,8,512]{3,2,1,0:T(8,128)S(1)}, f32[1,1,8,512]{3,2,1,0:T(8,128)}, u32[]{:S(2)}) copy-start(f32[1,1,8,512]{3,2,1,0:T(8,128)} %param.17) | copy-start | bytes 49156

commit v2 on v1

--- a/solution.py
+++ b/solution.py
@@ -21,8 +21,8 @@
 
 
 def block_kernel(
-    n_shot, n_tx, n_ty, lag_ref, now_ref, prev_ref, cour_ref, ridx_ref, hist_ref, green_ref,
-    last_ref, out_ref, em_ref,
+    n_shot, n_tx, n_ty, lag_ref, now_ref, prev_ref, cour_far, ridx_far, hist_ref, green_ref,
+    last_ref, out_ref, em_ref, cour_ref, ridx_ref,
     field, ysend, yrecv, pick_xy, pick_z,
     hist_all, rec, rec_all, early, blocks, xpart, xrecv, zpart, zsend, zrecv,
     load_sem, send_sem, recv_sem, green_sem, hist_send, hist_recv, rec_send, rec_recv,
@@ -65,6 +65,9 @@
     loads = [
         pltpu.make_async_copy(prev_ref, field.at[0, :, pl.ds(1, ext_x)], load_sem.at[0]),
         pltpu.make_async_copy(now_ref, field.at[1, :, pl.ds(1, ext_x)], load_sem.at[1]),
+        pltpu.make_async_copy(cour_far, cour_ref, load_sem.at[2]),
+        pltpu.make_async_copy(ridx_far, ridx_ref, load_sem.at[3]),
+        pltpu.make_async_copy(hist_ref, hist_all.at[0], load_sem.at[4]),
     ]
     for load in loads + green_loads:
         load.start()
@@ -94,7 +97,6 @@
             device_id={"shot": (me + di) % n_shot}, device_id_type=mesh_id,
         )
 
-    hist_all[0] = hist_ref[...]
     rec[...] = jnp.zeros(rec.shape, jnp.float32)
 
     for side in range(4):
@@ -107,13 +109,6 @@
                     yrecv[slot, side - 2] = jnp.zeros((shots, ext_x, 1, depth), jnp.float32)
                 return carry
             lax.fori_loop(1, STEPS + 1, clear, 0)
-
-    cells = ridx_ref[...]
-    points = cells.shape[1]
-    rows = lax.broadcasted_iota(jnp.int32, (ext_x * ext_y, points), 0)
-    pick_xy[...] = jnp.where(rows == cells // depth, 1.0, 0.0).astype(jnp.bfloat16)
-    deep = lax.broadcasted_iota(jnp.int32, (depth, points), 0)
-    pick_z[...] = jnp.where(deep == cells % depth, 1.0, 0.0)
 
     def copy(slot, side):
         if side < 2:
@@ -140,38 +135,55 @@
         )
 
     def send(slot):
-        for side in range(2):
+        for side in (2, 3, 0, 1):
             @pl.when(there[side])
             def _():
                 copy(slot, side).start()
-        ysend[slot, 0] = field[slot, :, 1 : ext_x + 1, 0:1, :]
-        ysend[slot, 1] = field[slot, :, 1 : ext_x + 1, ext_y - 1 : ext_y, :]
-        for side in range(2, 4):
-            @pl.when(there[side])
-            def _():
-                copy(slot, side).start()
-
-    for load in loads:
+
+    for load in loads[1:]:
         load.wait()
+    ysend[1, 0] = field[1, :, 1 : ext_x + 1, 0:1, :]
+    ysend[1, 1] = field[1, :, 1 : ext_x + 1, ext_y - 1 : ext_y, :]
     pl.semaphore_wait(barrier, n_tx - 1 + len(offsets))
     send(1)
     for di in range(1, n_shot):
         share(hist_all, hist_send, hist_recv, di).start()
 
+    cells = ridx_ref[...]
+    points = cells.shape[1]
+    rows = lax.broadcasted_iota(jnp.int32, (ext_x * ext_y, points), 0)
+    pick_xy[...] = jnp.where(rows == cells // depth, 1.0, 0.0).astype(jnp.bfloat16)
+    deep = lax.broadcasted_iota(jnp.int32, (depth, points), 0)
+    pick_z[...] = jnp.where(deep == cells % depth, 1.0, 0.0)
+
+    loads[0].wait()
+
     part = 4 if ext_x % 4 == 0 else 1
     shape = (part, ext_y, depth)
     at_y = lax.broadcasted_iota(jnp.int32, shape, 1)
     at_z = lax.broadcasted_iota(jnp.int32, shape, 2)
 
-    def advance(slot):
+    def inner(slot):
         def one_shot(s, carry):
             for x0 in range(0, ext_x, part):
                 centre = field[slot, s, x0 + 1 : x0 + 1 + part]
-                total = field[slot, s, x0 : x0 + part] + field[slot, s, x0 + 2 : x0 + 2 + part]
-                low = jnp.broadcast_to(yrecv[slot, 0, s, x0 : x0 + part], shape)
-                high = jnp.broadcast_to(yrecv[slot, 1, s, x0 : x0 + part], shape)
-                total += jnp.where(at_y == 0, low, pltpu.roll(centre, 1, 1))
-                total += jnp.where(at_y == ext_y - 1, high, pltpu.roll(centre, ext_y - 1, 1))
+                if x0 == 0:
+                    below = [jnp.zeros((1, ext_y, depth), jnp.float32)]
+                    if part > 1:
+                        below.append(field[slot, s, 1:part])
+                    below = jnp.concatenate(below, 0)
+                else:
+                    below = field[slot, s, x0 : x0 + part]
+                if x0 + part == ext_x:
+                    above = [jnp.zeros((1, ext_y, depth), jnp.float32)]
+                    if part > 1:
+                        above.insert(0, field[slot, s, x0 + 2 : ext_x + 1])
+                    above = jnp.concatenate(above, 0)
+                else:
+                    above = field[slot, s, x0 + 2 : x0 + 2 + part]
+                total = below + above
+                total += jnp.where(at_y == 0, 0.0, pltpu.roll(centre, 1, 1))
+                total += jnp.where(at_y == ext_y - 1, 0.0, pltpu.roll(centre, ext_y - 1, 1))
                 total += jnp.where(at_z == 0, 0.0, pltpu.roll(centre, 1, 2))
                 total += jnp.where(at_z == depth - 1, 0.0, pltpu.roll(centre, depth - 1, 2))
                 before = field[slot - 1, s, x0 + 1 : x0 + 1 + part]
@@ -182,6 +194,22 @@
             return carry
         lax.fori_loop(0, shots, one_shot, 0)
 
+    def border(slot, pack):
+        for side in range(2):
+            arrive(slot, side)
+            halo, edge = (0, 1) if side == 0 else (ext_x + 1, ext_x)
+            field[slot + 1, :, edge] += cour_ref[edge - 1][None] * field[slot, :, halo]
+        for side in range(2, 4):
+            arrive(slot, side)
+            edge = 0 if side == 2 else ext_y - 1
+            speed = cour_ref[:, edge : edge + 1, :]
+            for s in range(shots):
+                row = field[slot + 1, s, 1 : ext_x + 1, edge : edge + 1, :]
+                row += speed * yrecv[slot, side - 2, s]
+                if pack:
+                    ysend[slot + 1, side - 2, s] = row
+                field[slot + 1, s, 1 : ext_x + 1, edge : edge + 1, :] = row
+
     def sample(slot):
         for s in range(shots):
             tile = field[slot, s, 1 : ext_x + 1].reshape(ext_x * ext_y, depth).astype(jnp.bfloat16)
@@ -192,11 +220,10 @@
                 found * pick_z[...], axis=0, keepdims=True
             )
 
-    def arrive(slot):
-        for side in range(4):
-            @pl.when(there[side])
-            def _():
-                landing(slot, side).wait_recv()
+    def arrive(slot, side):
+        @pl.when(there[side])
+        def _():
+            landing(slot, side).wait_recv()
 
     first_early = 2
 
@@ -207,10 +234,10 @@
         )
 
     def step(slot, carry):
-        arrive(slot)
-        advance(slot)
+        border(slot, True)
         send(slot + 1)
         sample(slot + 1)
+        inner(slot + 1)
 
         @pl.when(slot == first_early)
         def _():
@@ -224,6 +251,7 @@
             early_part(slot - first_early)
         return carry
 
+    inner(1)
     lax.fori_loop(1, STEPS, step, 0)
     for m in range(STEPS - first_early, n_tx):
         early_part(m)
@@ -231,8 +259,7 @@
     rec_all[0] = rec[...].astype(jnp.bfloat16)
     for di in range(1, n_shot):
         share(rec_all, rec_send, rec_recv, di).start()
-    arrive(STEPS)
-    advance(STEPS)
+    border(STEPS, False)
     stores = [
         pltpu.make_async_copy(field.at[STEPS, :, pl.ds(1, ext_x)], last_ref, load_sem.at[0]),
         pltpu.make_async_copy(field.at[STEPS + 1, :, pl.ds(1, ext_x)], out_ref, load_sem.at[1]),
@@ -336,10 +363,12 @@
             jax.ShapeDtypeStruct((n_shot, rows_each, each), jnp.float32),
         ),
         in_specs=[
-            pl.BlockSpec(memory_space=pltpu.SMEM), far, far, whole, whole, whole, far
-        ],
+            pl.BlockSpec(memory_space=pltpu.SMEM)
+        ] + [pl.BlockSpec(memory_space=pltpu.HBM)] * 6,
         out_specs=(far, far, whole),
         scratch_shapes=[
+            pltpu.VMEM((ext_x, ext_y, depth), jnp.float32),
+            pltpu.VMEM((1, points), jnp.int32),
             pltpu.VMEM((STEPS + 2, shots, ext_x + 2, ext_y, depth), jnp.float32),
             pltpu.VMEM((STEPS + 1, 2, shots, ext_x, 1, depth), jnp.float32),
             pltpu.VMEM((STEPS + 1, 2, shots, ext_x, 1, depth), jnp.float32),
@@ -355,7 +384,7 @@
             pltpu.VMEM((n_ty, n_shot, rows_each, each), jnp.float32),
             pltpu.VMEM((n_ty, n_shot, rows_each, each), jnp.bfloat16),
             pltpu.VMEM((n_ty, n_shot, rows_each, each), jnp.bfloat16),
-            dma((2,)),
+            dma((5,)),
             dma((STEPS + 1, 4)),
             dma((STEPS + 1, 4)),
             dma((groups, n_tx)),
@@ -374,35 +403,66 @@
     )(lag_delay, wave_now, wave_prev, courant, ridx, history, green)
 
 
-def inject_kernel(wave_ref, cells_ref, weights_ref, last_ref, out_ref):
+def inject_kernel(
+    previous_ref, wave_ref, cells_ref, weights_ref, columns_ref,
+    out_ref, last_ref, emission_ref, done, sems,
+):
     shots, ext_x, ext_y, depth = wave_ref.shape
-    corners, points = cells_ref.shape
-    rows = lax.broadcasted_iota(jnp.int32, (ext_x * ext_y, points), 0)
-    deep = lax.broadcasted_iota(jnp.int32, (depth, points), 0)
+    n_shot, rows_each, each = columns_ref.shape
+    corners = cells_ref.shape[0]
+    keep = pltpu.make_async_copy(previous_ref, last_ref, sems.at[shots])
+    keep.start()
+    for s in range(shots):
+        for t in range(STEPS):
+            for i in range(n_shot):
+                emission_ref[s, t, 0, :, i * each : (i + 1) * each] = columns_ref[
+                    i, s * STEPS + t : s * STEPS + t + 1, :
+                ]
+    rows = lax.broadcasted_iota(jnp.int32, (ext_x * ext_y, each), 0)
+    deep = lax.broadcasted_iota(jnp.int32, (depth, each), 0)
     totals = [wave_ref[s].reshape(ext_x * ext_y, depth) for s in range(shots)]
     for k in range(corners):
-        cells = cells_ref[k : k + 1, :]
-        pick = jnp.where(rows == cells // depth, 1.0, 0.0).astype(jnp.bfloat16)
-        here = deep == cells % depth
-        values = weights_ref[k : k + 1, :] * last_ref[...]
-        for s in range(shots):
-            spread = jnp.where(here, values[s : s + 1, :], 0.0).astype(jnp.bfloat16)
-            totals[s] += lax.dot_general(
-                pick, spread, (((1,), (1,)), ((), ())), preferred_element_type=jnp.float32
-            )
+        for i in range(n_shot):
+            span = slice(i * each, (i + 1) * each)
+            cells = cells_ref[k : k + 1, span]
+            pick = jnp.where(rows == cells // depth, 1.0, 0.0).astype(jnp.bfloat16)
+            here = deep == cells % depth
+            for s in range(shots):
+                final = (s + 1) * STEPS - 1
+                values = weights_ref[k : k + 1, span] * columns_ref[i, final : final + 1, :]
+                spread = jnp.where(here, values, 0.0).astype(jnp.bfloat16)
+                totals[s] += lax.dot_general(
+                    pick, spread, (((1,), (1,)), ((), ())), preferred_element_type=jnp.float32
+                )
+    stores = []
     for s in range(shots):
-        out_ref[s] = totals[s].reshape(ext_x, ext_y, depth)
-
-
-def inject(wave, cells, weights, last):
+        done[s] = totals[s].reshape(ext_x, ext_y, depth)
+        stores.append(pltpu.make_async_copy(done.at[s], out_ref.at[s], sems.at[s]))
+        stores[-1].start()
+    for store in stores + [keep]:
+        store.wait()
+
+
+def inject(previous, wave, cells, weights, columns):
     whole = pl.BlockSpec(memory_space=pltpu.VMEM)
+    far = pl.BlockSpec(memory_space=pl.ANY)
+    shots = wave.shape[0]
+    points = cells.shape[1]
     return pl.pallas_call(
         inject_kernel,
-        out_shape=jax.ShapeDtypeStruct(wave.shape, jnp.float32),
-        in_specs=[whole] * 4,
-        out_specs=whole,
+        out_shape=(
+            jax.ShapeDtypeStruct(wave.shape, jnp.float32),
+            jax.ShapeDtypeStruct(wave.shape, jnp.float32),
+            jax.ShapeDtypeStruct((shots, STEPS, 1, 1, points), jnp.float32),
+        ),
+        in_specs=[far] + [whole] * 4,
+        out_specs=(far, far, whole),
+        scratch_shapes=[
+            pltpu.VMEM(wave.shape, jnp.float32),
+            pltpu.SemaphoreType.DMA((shots + 1,)),
+        ],
         compiler_params=pltpu.CompilerParams(vmem_limit_bytes=40 * MIB),
-    )(wave, cells, weights, last)
+    )(previous, wave, cells, weights, columns)
 
 
 def local(
@@ -414,15 +474,13 @@
         n_shot, n_tx, n_ty, lag_delay, wave_now, wave_prev, courant,
         rec_index.reshape(1, -1), rec_history.reshape(shots_here * HIST, -1), green,
     )
-    owned = columns.reshape(n_shot, shots_here, STEPS, -1).transpose(1, 2, 0, 3)
-    owned = owned.reshape(shots_here, STEPS, -1)
-    wave_out = inject(
+    return inject(
+        previous,
         current,
         emit_cells.reshape(emit_cells.shape[-2:]),
         emit_weights.reshape(emit_weights.shape[-2:]),
-        owned[:, STEPS - 1, :],
+        columns,
     )
-    return (wave_out, previous, owned.reshape(shots_here, STEPS, 1, 1, -1))
 
 
 def solution(mesh):

time: 60.4 us -> 55.9 us (0.925)
  Pallas kernels: 53.7 us -> 50.9 us
  local copies, waits for them, and re-layouts: 5.73 us -> 4.04 us
    pallas_call x1, Pallas kernels: 50.6 us -> 47.1 us  [run_block(): pl.pallas_call(functools.partial(block_kernel, n_shot, n_tx, n_ty), out_s...]
    unnamed x15 -> x14, local copies, waits for them, and re-layouts: 4.83 us -> 4.04 us
    another operation x1 -> x0, local copies, waits for them, and re-layouts: 0.73 us -> none  [local(): return (wave_out, previous, owned.reshape(shots_here, STEPS, 1, 1, -1))]
where the time goes in v2:
time: 55.9 us; the launch traced here: 55.6 us
  Pallas kernels  50.9 us (91%)
  local copies, waits for them, and re-layouts  4.04 us (7%)
  between operations  0.67 us (1%)
    pallas_call x1, Pallas kernels, run_block(): pl.pallas_call(functools.partial(block_kernel, n_shot, n_tx, n_ty), out_s...  47.1 us
    unnamed x14, local copies, waits for them, and re-layouts  4.04 us
    pallas_call x1, Pallas kernels, inject(): pl.pallas_call(inject_kernel, out_shape=(jax.ShapeDtypeStruct(wave.shape,...  3.75 us

profile of v2, /device:TPU:0, one launch (start us, length us, event | category | flops | bytes accessed | tf_op | source)
XLA Modules:
  0.0 55.6 jit_solution(2913754380377133905)
XLA Ops:
  0.6 0.0 copy-start
  0.6 1.0 %copy-done = f32[4,16,16,128]{3,2,1,0:T(8,128)S(1)} copy-done((f32[4,16,16,128]{3,2,1,0:T(8,128)S(1)}, f32[4,16,16,128]{3,2,1,0:T(8,128)}, u32[]{:S(2)}) %copy-start) | copy-done | bytes 524312
  1.7 0.0 copy-start.1
  1.7 0.9 %copy-done.1 = f32[16,16,128]{2,1,0:T(8,128)S(1)} copy-done((f32[16,16,128]{2,1,0:T(8,128)S(1)}, f32[16,16,128]{2,1,0:T(8,128)}, u32[]{:S(2)}) %copy-start.1) | copy-done | bytes 131096
  2.6 0.0 copy-start.2
  2.6 0.8 %copy-done.2 = bf16[4,8,1,1,512]{4,1,3,2,0:T(8,128)(2,1)S(1)} copy-done((bf16[4,8,1,1,512]{4,1,3,2,0:T(8,128)(2,1)S(1)}, bf16[4,8,1,1,512]{4,1,3,2,0:T(8,128)(2,1)}, u32[]{:S(2)}) %copy-start.2) | copy-done | bytes 32792
  3.3 0.0 copy-start.5
  3.3 0.7 %copy-done.5 = s32[1,1,512]{2,1,0:T(1,128)S(1)} copy-done((s32[1,1,512]{2,1,0:T(1,128)S(1)}, s32[1,1,512]{2,1,0:T(1,128)}, u32[]{:S(2)}) %copy-start.5) | copy-done | bytes 2072
  4.0 0.0 copy-start.6
  4.0 0.7 %copy-done.6 = s32[2]{0:T(128)S(1)} copy-done((s32[2]{0:T(128)S(1)}, s32[2]{0:T(128)}, u32[]{:S(2)}) %copy-start.6) | copy-done | bytes 32
  4.7 0.0 copy-start.3
  4.7 0.0 copy-start.4
  4.7 47.1 %shard_map.112 = (f32[4,16,16,128]{3,2,1,0:T(8,128)S(1)}, f32[4,16,16,128]{3,2,1,0:T(8,128)S(1)}, f32[2,32,256]{2,1,0:T(8,128)S(1)}) custom-call(s32[2]{0:T(128)S(1)} %copy-done.6, f32[4,16,16,128]{3,2,1,0:T(8,128)S(1)} %copy-done, f32[4,16,16,128]{3,2,1,0:T(8,128)} %prev_ref.1, f32[16,16,128]{2,1,0:T(8,128)S(1)} %copy-done.1, s32[1,512]{1,0:T(1,128)S(1)} %bitcast.7, ...), custom_call_target="tpu_custom_call" | custom-call | tf_op jit(solution)/shard_map/pallas_call | solution.py:358
  51.8 0.0 copy-done.3
  51.8 0.0 copy-done.4
  51.9 3.8 %shard_map.113 = (f32[4,16,16,128]{3,2,1,0:T(8,128)}, f32[4,16,16,128]{3,2,1,0:T(8,128)}, f32[4,8,1,1,512]{4,3,2,1,0:T(1,128)}) custom-call(f32[4,16,16,128]{3,2,1,0:T(8,128)S(1)} %get-tuple-element.6.previous_ref, f32[4,16,16,128]{3,2,1,0:T(8,128)S(1)} %get-tuple-element.7.wave_ref, s32[8,512]{1,0:T(8,128)S(1)} %bitcast.5, f32[8,512]{1,0:T(8,128)S(1)} %bitcast.6, ...), custom_call_target="tpu_custom_call" | custom-call | tf_op jit(solution)/shard_map/pallas_call | solution.py:451
Async XLA Ops:
  0.6 1.0 %copy-start = (f32[4,16,16,128]{3,2,1,0:T(8,128)S(1)}, f32[4,16,16,128]{3,2,1,0:T(8,128)}, u32[]{:S(2)}) copy-start(f32[4,16,16,128]{3,2,1,0:T(8,128)} %now_ref.1) | copy-start | bytes 1572868
  1.7 0.9 %copy-start.1 = (f32[16,16,128]{2,1,0:T(8,128)S(1)}, f32[16,16,128]{2,1,0:T(8,128)}, u32[]{:S(2)}) copy-start(f32[16,16,128]{2,1,0:T(8,128)} %cour_far.1) | copy-start | bytes 393220
  2.6 0.8 %copy-start.2 = (bf16[4,8,1,1,512]{4,1,3,2,0:T(8,128)(2,1)S(1)}, bf16[4,8,1,1,512]{4,1,3,2,0:T(8,128)(2,1)}, u32[]{:S(2)}) copy-start(bf16[4,8,1,1,512]{4,1,3,2,0:T(8,128)(2,1)} %param.13) | copy-start | bytes 98308
  3.3 0.7 %copy-start.5 = (s32[1,1,512]{2,1,0:T(1,128)S(1)}, s32[1,1,512]{2,1,0:T(1,128)}, u32[]{:S(2)}) copy-start(s32[1,1,512]{2,1,0:T(1,128)} %param.12) | copy-start | bytes 6148
  4.0 0.7 %copy-start.6 = (s32[2]{0:T(128)S(1)}, s32[2]{0:T(128)}, u32[]{:S(2)}) copy-start(s32[2]{0:T(128)} %lag_ref.1) | copy-start | bytes 28
  4.7 47.2 %copy-start.3 = (s32[1,1,8,512]{3,2,1,0:T(8,128)S(1)}, s32[1,1,8,512]{3,2,1,0:T(8,128)}, u32[]{:S(2)}) copy-start(s32[1,1,8,512]{3,2,1,0:T(8,128)} %param.16) | copy-start | bytes 49156
  4.7 47.2 %copy-start.4 = (f32[1,1,8,512]{3,2,1,0:T(8,128)S(1)}, f32[1,1,8,512]{3,2,1,0:T(8,128)}, u32[]{:S(2)}) copy-start(f32[1,1,8,512]{3,2,1,0:T(8,128)} %param.17) | copy-start | bytes 49156

commit v3 on v2

--- a/solution.py
+++ b/solution.py
@@ -398,20 +398,34 @@
             dma((n_ty, n_shot)),
         ],
         compiler_params=pltpu.CompilerParams(
-            collective_id=0, has_side_effects=True, vmem_limit_bytes=52 * MIB
+            collective_id=0, has_side_effects=True, vmem_limit_bytes=60 * MIB
         ),
     )(lag_delay, wave_now, wave_prev, courant, ridx, history, green)
 
 
 def inject_kernel(
-    previous_ref, wave_ref, cells_ref, weights_ref, columns_ref,
-    out_ref, last_ref, emission_ref, done, sems,
+    previous_ref, wave_far, cells_far, weights_far, columns_far,
+    out_ref, last_ref, emission_ref,
+    wave_ref, cells_ref, weights_ref, columns_ref, sems, load_sem,
 ):
     shots, ext_x, ext_y, depth = wave_ref.shape
     n_shot, rows_each, each = columns_ref.shape
     corners = cells_ref.shape[0]
     keep = pltpu.make_async_copy(previous_ref, last_ref, sems.at[shots])
+    loads = [
+        pltpu.make_async_copy(src, dst, load_sem.at[i])
+        for i, (src, dst) in enumerate((
+            (columns_far, columns_ref),
+            (cells_far, cells_ref),
+            (weights_far, weights_ref),
+            (wave_far, wave_ref),
+        ))
+    ]
+    for load in loads:
+        load.start()
     keep.start()
+    for load in loads[:3]:
+        load.wait()
     for s in range(shots):
         for t in range(STEPS):
             for i in range(n_shot):
@@ -420,7 +434,7 @@
                 ]
     rows = lax.broadcasted_iota(jnp.int32, (ext_x * ext_y, each), 0)
     deep = lax.broadcasted_iota(jnp.int32, (depth, each), 0)
-    totals = [wave_ref[s].reshape(ext_x * ext_y, depth) for s in range(shots)]
+    totals = [jnp.zeros((ext_x * ext_y, depth), jnp.float32) for s in range(shots)]
     for k in range(corners):
         for i in range(n_shot):
             span = slice(i * each, (i + 1) * each)
@@ -435,9 +449,10 @@
                     pick, spread, (((1,), (1,)), ((), ())), preferred_element_type=jnp.float32
                 )
     stores = []
+    loads[3].wait()
     for s in range(shots):
-        done[s] = totals[s].reshape(ext_x, ext_y, depth)
-        stores.append(pltpu.make_async_copy(done.at[s], out_ref.at[s], sems.at[s]))
+        wave_ref[s] += totals[s].reshape(ext_x, ext_y, depth)
+        stores.append(pltpu.make_async_copy(wave_ref.at[s], out_ref.at[s], sems.at[s]))
         stores[-1].start()
     for store in stores + [keep]:
         store.wait()
@@ -455,13 +470,17 @@
             jax.ShapeDtypeStruct(wave.shape, jnp.float32),
             jax.ShapeDtypeStruct((shots, STEPS, 1, 1, points), jnp.float32),
         ),
-        in_specs=[far] + [whole] * 4,
+        in_specs=[pl.BlockSpec(memory_space=pltpu.HBM)] * 5,
         out_specs=(far, far, whole),
         scratch_shapes=[
             pltpu.VMEM(wave.shape, jnp.float32),
+            pltpu.VMEM(cells.shape, jnp.int32),
+            pltpu.VMEM(weights.shape, jnp.float32),
+            pltpu.VMEM(columns.shape, jnp.float32),
             pltpu.SemaphoreType.DMA((shots + 1,)),
+            pltpu.SemaphoreType.DMA((4,)),
         ],
-        compiler_params=pltpu.CompilerParams(vmem_limit_bytes=40 * MIB),
+        compiler_params=pltpu.CompilerParams(vmem_limit_bytes=60 * MIB),
     )(previous, wave, cells, weights, columns)
 
 

time: 55.9 us -> 66.9 us (1.20)
  Pallas kernels: 50.9 us -> 66.1 us
  local copies, waits for them, and re-layouts: 4.04 us -> 0 us
    pallas_call x1, Pallas kernels: 3.75 us -> 17.7 us  [inject(): pl.pallas_call(inject_kernel, out_shape=(jax.ShapeDtypeStruct(wave.shape,...]
    unnamed x14 -> x0, local copies, waits for them, and re-layouts: 4.04 us -> none
    pallas_call x1, Pallas kernels: 47.1 us -> 48.4 us  [run_block(): pl.pallas_call(functools.partial(block_kernel, n_shot, n_tx, n_ty), out_s...]
where the time goes in v3:
time: 66.9 us; the launch traced here: 66.8 us
  Pallas kernels  66.1 us (99%)
    pallas_call x1, Pallas kernels, run_block(): pl.pallas_call(functools.partial(block_kernel, n_shot, n_tx, n_ty), out_s...  48.4 us
    pallas_call x1, Pallas kernels, inject(): pl.pallas_call(inject_kernel, out_shape=(jax.ShapeDtypeStruct(wave.shape,...  17.7 us

profile of v3, /device:TPU:0, one launch (start us, length us, event | category | flops | bytes accessed | tf_op | source)
XLA Modules:
  0.0 66.8 jit_solution(524667883319888013)
XLA Ops:
  0.6 48.4 %shard_map.112 = (f32[4,16,16,128]{3,2,1,0:T(8,128)}, f32[4,16,16,128]{3,2,1,0:T(8,128)}, f32[2,32,256]{2,1,0:T(8,128)}) custom-call(s32[2]{0:T(128)} %lag_ref.1, f32[4,16,16,128]{3,2,1,0:T(8,128)} %now_ref.1, f32[4,16,16,128]{3,2,1,0:T(8,128)} %prev_ref.1, f32[16,16,128]{2,1,0:T(8,128)} %cour_far.1, s32[1,512]{1,0:T(1,128)} %bitcast.7, ...), custom_call_target="tpu_custom_call" | custom-call | tf_op jit(solution)/shard_map/pallas_call | solution.py:358
  49.1 17.7 %shard_map.113 = (f32[4,16,16,128]{3,2,1,0:T(8,128)}, f32[4,16,16,128]{3,2,1,0:T(8,128)}, f32[4,8,1,1,512]{4,3,2,1,0:T(1,128)}) custom-call(f32[4,16,16,128]{3,2,1,0:T(8,128)} %get-tuple-element.6.previous_ref, f32[4,16,16,128]{3,2,1,0:T(8,128)} %get-tuple-element.7.wave_far, s32[8,512]{1,0:T(8,128)} %bitcast.5, f32[8,512]{1,0:T(8,128)} %bitcast.6, ...), custom_call_target="tpu_custom_call" | custom-call | tf_op jit(solution)/shard_map/pallas_call | solution.py:466
